TPU v7x, 32 devices: a whole 2x2x4 slice. The times are simulated.
32 devices in a mesh: pool: 32 (over z, y, x, core).
Axes of the slice: x: 2, y: 2, z: 4, core: 2. Of those that a mesh axis runs over, the one named last changes fastest.
Arguments:
- queries: bfloat16 [32, 2, 3584], P('pool'), may hold values from -120 to 120
- kv_pool: bfloat16 [1024, 256, 2, 512], P('pool'), may hold values from -6 to 6
- lengths: int32 [32], P('pool'), may hold values from 1 to 8190, 131072 in all
- block_table: int32 [1024], P('pool'), may hold values from 0 to 1023, as said below
Outputs:
- attended: bfloat16 [32, 2, 3584], P('pool')
Inputs may be any that keep to these rules, and one draw needn't show every extreme that they name: `block_table`: a permutation of the pool blocks; with the requests numbered in groups of 1 per owner index o and G groups, the entry at place j of the 32 entries of group o is a block numbered from ((o + s_j) mod G) * 32 to that + 31, where s_j = (j * G) // 32, except s_0 = 1 when G > 32. The pool holds positions 0 to lengths + 1 of each request.
All inputs are finite; a program needn't handle non-finite values. No bound on the sum of `lengths` on one device may be relied on, other than what follows from the above.
Results may differ from a plain program's by a relative error of at most 0.0095.
Values may be sent and summed in bfloat16 or wider, within the bound.
A program may use at most 192 MiB of HBM per device.

v0:
```python
import functools

import jax
import jax.numpy as jnp
from jax import lax
from jax.experimental import pallas as pl
from jax.experimental.pallas import tpu as pltpu
from jax.sharding import PartitionSpec as P

KVH = 4
GROUP = 7
HEAD = 128
BLOCK = 256
ROWS = 16 * KVH
PLANE = 4
CORES = 2
M_ROW, L_ROW, L_LOW_ROW = 14, 15, 30
MASKED = -1e30
FLOOR = -1e20
UNROLL = 4
SCALE = 1.0 / HEAD**0.5
MESH = pl.DeviceIdType.MESH


def places():
    me = lax.axis_index("pool")
    chip = lax.div(me, CORES)
    z = lax.div(chip, PLANE)
    return me, z, chip - z * PLANE, me - chip * CORES


def wrap(value, size):
    return jnp.where(value >= size, value - size, value)


def remote(src, dst, s, r, to):
    return pltpu.make_async_remote_copy(
        src_ref=src, dst_ref=dst, send_sem=s, recv_sem=r, device_id=to, device_id_type=MESH
    )


def greet(peers):
    barrier = pltpu.get_barrier_semaphore()
    for peer in peers:
        pl.semaphore_signal(barrier, inc=1, device_id=peer, device_id_type=MESH)
    return lambda: pl.semaphore_wait(barrier, len(peers))


class Grid:
    def __init__(self, n):
        self.me, self.z, self.p, self.c = places()
        self.depth = n // (PLANE * CORES)
        self.other = 1 - self.c
        self.line_to = [wrap(self.z + i, self.depth) for i in range(self.depth)]
        self.line_from = [wrap(self.z + self.depth - i, self.depth) for i in range(self.depth)]
        self.plane_to = [wrap(self.p + i, PLANE) for i in range(PLANE)]
        self.plane_from = [wrap(self.p + PLANE - i, PLANE) for i in range(PLANE)]
        self.sent = []

    def at(self, z, p, c):
        return ((z * PLANE + p) * CORES + c,)

    def line(self, z):
        return self.at(z, self.p, self.c)

    def plane(self, p):
        return self.at(self.z, p, self.c)

    def core(self):
        return self.at(self.z, self.p, self.other)

    def peers(self):
        peers = [self.line(z) for z in self.line_to[1:]]
        return peers + [self.plane(p) for p in self.plane_to[1:]] + [self.core()]

    def go(self, src, dst, s, r, to):
        copy = remote(src, dst, s, r, to)
        copy.start()
        self.sent.append(copy)

    def arrive(self, dst, s, r):
        remote(dst, dst, s, r, self.core()).wait_recv()

    def finish(self):
        for copy in self.sent:
            copy.wait_send()


def gather_kernel(
    n, width,
    query_ref, lengths_ref, table_ref, every_query, meta,
    spread, held_query, length_scalar, table_scalar, small_sem,
    meta_line_s, meta_line_r, meta_plane_s, meta_plane_r, meta_core_s, meta_core_r,
    query_line_s, query_line_r, query_plane_s, query_plane_r, query_core_s, query_core_r,
):
    g = Grid(n)
    zz, pp, cc, depth = g.z, g.p, g.c, g.depth
    greeted = greet(g.peers())
    small = [
        pltpu.make_async_copy(lengths_ref, length_scalar, small_sem.at[0]),
        pltpu.make_async_copy(table_ref, table_scalar, small_sem.at[1]),
        pltpu.make_async_copy(query_ref, held_query, small_sem.at[2]),
    ]
    for copy in small:
        copy.start()

    spread[...] = jnp.zeros_like(spread)
    for copy in small:
        copy.wait()
    own_query = held_query[0].astype(jnp.float32)
    for h in range(KVH * GROUP):
        row = 16 * (h // GROUP) + 2 * (h % GROUP)
        spread[row : row + 2, :] = own_query[:, h * HEAD : (h + 1) * HEAD]
    every_query[zz, cc, pp] = spread[...].astype(jnp.bfloat16)
    lane = lax.broadcasted_iota(jnp.int32, (1, HEAD), 1)
    own_meta = jnp.where(lane == width, length_scalar[0], 0)
    for j in range(width):
        own_meta = jnp.where(lane == j, table_scalar[j], own_meta)
    meta[cc, pp, zz] = own_meta
    greeted()

    def query_to_plane(i):
        ref = every_query.at[g.line_from[i], cc, pp]
        for d in range(1, PLANE):
            g.go(ref, ref, query_plane_s.at[i, d - 1], query_plane_r.at[i, d - 1], g.plane(g.plane_to[d]))

    for i in range(1, depth):
        ref = every_query.at[zz, cc, pp]
        g.go(ref, ref, query_line_s.at[i - 1], query_line_r.at[i - 1], g.line(g.line_to[i]))
    for i in range(1, depth):
        ref = meta.at[cc, pp, zz]
        g.go(ref, ref, meta_line_s.at[i - 1], meta_line_r.at[i - 1], g.line(g.line_to[i]))
    query_to_plane(0)
    for i in range(1, depth):
        g.arrive(every_query.at[g.line_from[i], cc, pp], query_line_s.at[i - 1], query_line_r.at[i - 1])
        query_to_plane(i)
    for i in range(1, depth):
        g.arrive(meta.at[cc, pp, g.line_from[i]], meta_line_s.at[i - 1], meta_line_r.at[i - 1])
    for d in range(1, PLANE):
        ref = meta.at[cc, pp]
        g.go(ref, ref, meta_plane_s.at[d - 1], meta_plane_r.at[d - 1], g.plane(g.plane_to[d]))
    for i in range(depth):
        for d in range(1, PLANE):
            g.arrive(every_query.at[g.line_from[i], cc, g.plane_from[d]],
                     query_plane_s.at[i, d - 1], query_plane_r.at[i, d - 1])
        ref = every_query.at[g.line_from[i], cc]
        g.go(ref, ref, query_core_s.at[i], query_core_r.at[i], g.core())
    for d in range(1, PLANE):
        g.arrive(meta.at[cc, g.plane_from[d]], meta_plane_s.at[d - 1], meta_plane_r.at[d - 1])
    ref = meta.at[cc]
    g.go(ref, ref, meta_core_s.at[0], meta_core_r.at[0], g.core())
    for i in range(depth):
        g.arrive(every_query.at[g.line_from[i], g.other], query_core_s.at[i], query_core_r.at[i])
    g.arrive(meta.at[g.other], meta_core_s.at[0], meta_core_r.at[0])
    g.finish()


def state_ids():
    row_id = lax.broadcasted_iota(jnp.int32, (ROWS, HEAD), 0)
    return row_id, row_id == lax.broadcasted_iota(jnp.int32, (ROWS, HEAD), 1)


def encode(numer, peak, total):
    row_id, _ = state_ids()
    high = total.astype(jnp.bfloat16).astype(jnp.float32)
    numer = jnp.where(row_id == M_ROW, peak, numer)
    numer = jnp.where(row_id == L_ROW, high, numer)
    return jnp.where(row_id == L_LOW_ROW, total - high, numer)


def attend_kernel(
    n, slots, width,
    query_ref, meta_ref, pool_ref, out_ref,
    kv, columns, meta_scalar, held_at, held_limit, count_ref, kv_sem, scalar_sem,
):
    me = lax.axis_index("pool")
    stride = n // width
    to_scalar = pltpu.make_async_copy(meta_ref, meta_scalar, scalar_sem)
    to_scalar.start()
    row = lax.broadcasted_iota(jnp.int32, (2 * BLOCK, HEAD), 0)
    lane = lax.broadcasted_iota(jnp.int32, (2 * BLOCK, HEAD), 1)
    columns[...] = jnp.where(row % 2 == 0, row - 2 * (lane % 2), 1 << 24)
    row_id, _ = state_ids()
    empty = jnp.where(row_id == M_ROW, FLOOR, jnp.zeros((ROWS, HEAD), jnp.float32)).astype(out_ref.dtype)
    for request in range(n):
        out_ref[request] = empty
    depth = n // (PLANE * CORES)
    assert (PLANE, CORES) == (4, 2) and slots & (slots - 1) == 0

    def locate(place):
        step = place if stride == 1 else jnp.where(place == 0, 1, place * stride)
        request = me - step
        request = jnp.where(request < 0, request + n, request)
        return request >> 3, (request >> 1) & 3, request & 1

    to_scalar.wait()

    def pool_copies(index, slot):
        return [
            pltpu.make_async_copy(
                pool_ref.at[slot, :, :, pl.ds(k * HEAD, HEAD)], kv.at[k, index], kv_sem.at[k, index]
            )
            for k in range(KVH)
        ]

    count_ref[0] = 0

    @pl.loop(0, width)
    def _(place):
        z, p, c = locate(place)
        line = (c * PLANE + p) * depth + z
        length = meta_scalar[line, 0, width]

        @pl.when(place * BLOCK < length + 2)
        def _():
            index = count_ref[0]
            held_at[index] = (z * CORES + c) * PLANE + p
            held_limit[index] = 2 * (length + 1 - place * BLOCK)
            for copy in pool_copies(index, meta_scalar[line, 0, place] & (slots - 1)):
                copy.start()
            count_ref[0] = index + 1

    count = count_ref[0]
    rows = kv.reshape(KVH, slots, 2 * BLOCK, HEAD)

    lane_row = lax.broadcasted_iota(jnp.int32, (1, HEAD), 1)
    lane_group = lax.broadcasted_iota(jnp.int32, (HEAD, HEAD), 1) // 16

    def attend(indices):
        ats = [held_at[index] for index in indices]
        limit = jnp.where(lane_row < ROWS, held_limit[indices[0]], held_limit[indices[1]])
        pair = jnp.concatenate([query_ref[at] for at in ats], axis=0).astype(jnp.float32)
        pair = jnp.transpose(pair)
        scores = jnp.zeros((2 * BLOCK, HEAD), jnp.float32)
        for r in range(2):
            for k in range(0, KVH, 2):
                block = jnp.concatenate([rows[k, indices[r]], rows[k + 1, indices[r]]], axis=1)
                query = jnp.concatenate(
                    [jnp.where(lane_group == r * KVH + h, pair, 0.0) for h in (k, k + 1)], axis=0
                )
                scores += jnp.dot(block, query.astype(jnp.bfloat16), preferred_element_type=jnp.float32)
        scores = jnp.where(columns[...] < limit, scores * SCALE, MASKED)
        peak = jnp.maximum(jnp.max(scores, axis=0, keepdims=True), FLOOR)
        peak = peak.astype(jnp.bfloat16).astype(jnp.float32)
        unscaled = jnp.exp(scores - peak)
        total = jnp.sum(unscaled, axis=0, keepdims=True)
        shifted = pltpu.roll(unscaled.reshape(2 * BLOCK // 8, 8, HEAD), 1, 1).reshape(2 * BLOCK, HEAD)
        weights = jnp.transpose(shifted.astype(jnp.bfloat16))
        states = []
        for r in range(2):
            numers = []
            for k in range(0, KVH, 2):
                block = jnp.concatenate([rows[k, indices[r]], rows[k + 1, indices[r]]], axis=1)
                base = r * ROWS + 16 * k
                both = jnp.dot(weights[base : base + 32], block, preferred_element_type=jnp.float32)
                numers += [both[:16, :HEAD], both[16:, HEAD:]]
            if r == 1:
                peak, total = pltpu.roll(peak, ROWS, 1), pltpu.roll(total, ROWS, 1)
            state = encode(jnp.concatenate(numers, axis=0), peak, total)
            states.append((ats[r], state.astype(out_ref.dtype)))
        return states

    @pl.loop(0, (count + UNROLL - 1) // UNROLL)
    def _(step):
        for u in range(UNROLL):
            index = step * UNROLL + u

            @pl.when(index < count)
            def _():
                for copy in pool_copies(index, 0):
                    copy.wait()

        indices = [jnp.minimum(step * UNROLL + u, count - 1) for u in range(UNROLL)]
        done = [attend(indices[u : u + 2]) for u in range(0, UNROLL, 2)]
        for at, state in sum(done, []):
            out_ref[at] = state


def reduce_kernel(
    n, part_ref, out_ref,
    spread, core_recv, plane_send, plane_recv, plane_own, line_send, line_recv, line_own,
    core_s, core_r, plane_s, plane_r, line_s, line_r,
):
    g = Grid(n)
    depth = g.depth
    greet(g.peers())()
    _, eye = state_ids()

    def as_column(vector):
        return jnp.sum(jnp.where(eye, vector, 0.0), axis=1, keepdims=True)

    def merge(states):
        states = [s.astype(jnp.float32) for s in states]
        peaks = [s[M_ROW : M_ROW + 1] for s in states]
        totals = [s[L_ROW : L_ROW + 1] + s[L_LOW_ROW : L_LOW_ROW + 1] for s in states]
        peak = functools.reduce(jnp.maximum, peaks)
        shrink = [jnp.exp(p - peak) for p in peaks]
        total = sum(a * b for a, b in zip(shrink, totals))
        numer = sum(as_column(a) * s for a, s in zip(shrink, states))
        return numer, peak, total

    order = list(range(1, depth)) + [0]
    for i in order:
        g.go(part_ref.at[g.line_from[i], g.other], core_recv.at[i], core_s.at[i], core_r.at[i], g.core())

    def reduce_core(i):
        g.arrive(core_recv.at[i], core_s.at[i], core_r.at[i])
        for d in list(range(1, PLANE)) + [0]:
            p = g.plane_to[d]
            state = encode(*merge([part_ref[g.line_from[i], g.c, p], core_recv[i, p]]))
            if d == 0:
                plane_own[i] = state
            else:
                plane_send[i, d - 1] = state.astype(jnp.bfloat16)
                g.go(plane_send.at[i, d - 1], plane_recv.at[i, d - 1],
                     plane_s.at[i, d - 1], plane_r.at[i, d - 1], g.plane(p))

    def reduce_plane(i):
        for d in range(1, PLANE):
            g.arrive(plane_recv.at[i, d - 1], plane_s.at[i, d - 1], plane_r.at[i, d - 1])
        state = encode(*merge([plane_own[i]] + [plane_recv[i, d] for d in range(PLANE - 1)]))
        if i == 0:
            line_own[...] = state
        else:
            line_send[i - 1] = state.astype(jnp.bfloat16)
            g.go(line_send.at[i - 1], line_recv.at[i - 1], line_s.at[i - 1], line_r.at[i - 1],
                 g.line(g.line_from[i]))

    for i in order:
        reduce_core(i)
    for i in order:
        reduce_plane(i)
    for i in range(1, depth):
        g.arrive(line_recv.at[i - 1], line_s.at[i - 1], line_r.at[i - 1])
    numer, _, total = merge([line_own[...]] + [line_recv[i] for i in range(depth - 1)])
    spread[...] = numer / as_column(total)
    for h in range(KVH * GROUP):
        row = 16 * (h // GROUP) + 2 * (h % GROUP)
        out_ref[0, :, h * HEAD : (h + 1) * HEAD] = spread[row : row + 2, :].astype(jnp.bfloat16)
    g.finish()


def body(n, queries, kv_pool, lengths, block_table):
    slots, width = kv_pool.shape[0], block_table.shape[0]
    depth = n // (PLANE * CORES)
    state, bf16, f32, i32 = (ROWS, HEAD), jnp.bfloat16, jnp.float32, jnp.int32
    dma = pltpu.SemaphoreType.DMA
    vmem, anywhere = pl.BlockSpec(memory_space=pltpu.VMEM), pl.BlockSpec(memory_space=pl.ANY)
    far = pl.BlockSpec(memory_space=pltpu.HBM)
    every = jax.ShapeDtypeStruct((depth, CORES, PLANE) + state, bf16)
    meta_shape = (CORES, PLANE, depth, 1, HEAD)

    def params(**more):
        return pltpu.CompilerParams(has_side_effects=True, vmem_limit_bytes=48 * 1024 * 1024, **more)

    every_query, meta = pl.pallas_call(
        functools.partial(gather_kernel, n, width),
        out_shape=[every, jax.ShapeDtypeStruct(meta_shape, i32)],
        in_specs=[far, far, far],
        out_specs=[vmem, vmem],
        scratch_shapes=[
            pltpu.VMEM(state, f32), pltpu.VMEM(queries.shape, bf16),
            pltpu.SMEM((1,), i32), pltpu.SMEM((width,), i32), dma((3,)),
            dma((depth - 1,)), dma((depth - 1,)), dma((PLANE - 1,)), dma((PLANE - 1,)), dma((1,)), dma((1,)),
            dma((depth - 1,)), dma((depth - 1,)), dma((depth, PLANE - 1)), dma((depth, PLANE - 1)),
            dma((depth,)), dma((depth,)),
        ],
        compiler_params=params(collective_id=0),
    )(queries, lengths, block_table)
    parts = pl.pallas_call(
        functools.partial(attend_kernel, n, slots, width),
        out_shape=jax.ShapeDtypeStruct((n,) + state, bf16),
        in_specs=[vmem, anywhere, anywhere],
        out_specs=vmem,
        scratch_shapes=[
            pltpu.VMEM((KVH, slots, BLOCK, 2, HEAD), bf16),
            pltpu.VMEM((2 * BLOCK, HEAD), i32),
            pltpu.SMEM((n, 1, HEAD), i32),
            pltpu.SMEM((width,), i32), pltpu.SMEM((width,), i32), pltpu.SMEM((1,), i32),
            dma((KVH, slots)), dma,
        ],
        compiler_params=params(),
    )(every_query.reshape((n,) + state), meta.reshape(n, 1, HEAD), kv_pool)
    return pl.pallas_call(
        functools.partial(reduce_kernel, n),
        out_shape=jax.ShapeDtypeStruct(queries.shape, queries.dtype),
        in_specs=[vmem],
        out_specs=vmem,
        scratch_shapes=[
            pltpu.VMEM(state, f32),
            pltpu.VMEM((depth, PLANE) + state, bf16),
            pltpu.VMEM((depth, PLANE - 1) + state, bf16),
            pltpu.VMEM((depth, PLANE - 1) + state, bf16),
            pltpu.VMEM((depth,) + state, f32),
            pltpu.VMEM((depth - 1,) + state, bf16),
            pltpu.VMEM((depth - 1,) + state, bf16),
            pltpu.VMEM(state, f32),
            dma((depth,)), dma((depth,)), dma((depth, PLANE - 1)), dma((depth, PLANE - 1)),
            dma((depth - 1,)), dma((depth - 1,)),
        ],
        compiler_params=params(collective_id=1),
    )(parts.reshape(every.shape))


def solution(mesh):
    placed = (P("pool", None, None), P("pool", None, None, None), P("pool"), P("pool"))
    return jax.shard_map(
        functools.partial(body, mesh.shape["pool"]),
        mesh=mesh, in_specs=placed, out_specs=P("pool", None, None), check_vma=False,
    )
```

profile of v0, /device:TPU:0, one launch (start us, length us, event | category | flops | bytes accessed | tf_op | source)
XLA Modules:
  0.0 43.8 jit_solution(11337561067237539462)
XLA Ops:
  0.7 0.0 copy-start
  0.7 0.7 %copy-done = bf16[1,2,3584]{2,1,0:T(2,128)(2,1)S(1)} copy-done((bf16[1,2,3584]{2,1,0:T(2,128)(2,1)S(1)}, bf16[1,2,3584]{2,1,0:T(2,128)(2,1)}, u32[]{:S(2)}) %copy-start) | copy-done | bytes 14360
  1.4 0.0 copy-start.1
  1.4 0.7 %copy-done.1 = s32[32]{0:T(128)S(1)} copy-done((s32[32]{0:T(128)S(1)}, s32[32]{0:T(128)}, u32[]{:S(2)}) %copy-start.1) | copy-done | bytes 152
  2.0 13.9 %shard_map.46 = (bf16[4,2,4,64,128]{4,3,2,1,0:T(8,128)(2,1)S(1)}, s32[2,4,4,1,128]{4,3,2,1,0:T(1,128)S(1)}) custom-call(bf16[1,2,3584]{2,1,0:T(2,128)(2,1)S(1)} %copy-done, s32[1]{0:T(128)S(6)} %copy.6.lengths_ref, s32[32]{0:T(128)S(1)} %copy-done.1), custom_call_target="tpu_custom_call" | custom-call | tf_op jit(solution)/shard_map/pallas_call | solution.py:356
  15.9 15.0 %shard_map.47 = bf16[32,64,128]{2,1,0:T(8,128)(2,1)S(1)} custom-call(bf16[32,64,128]{2,1,0:T(8,128)(2,1)S(1)} %bitcast.4, s32[32,1,128]{2,1,0:T(1,128)S(1)} %bitcast.5, bf16[32,256,2,512]{3,2,1,0:T(2,128)(2,1)} %pool_ref.1), custom_call_target="tpu_custom_call" | custom-call | tf_op jit(solution)/shard_map/pallas_call | solution.py:370
  30.9 12.3 %shard_map.48 = bf16[1,2,3584]{2,1,0:T(2,128)(2,1)S(1)} custom-call(bf16[4,2,4,64,128]{4,3,2,1,0:T(8,128)(2,1)S(1)} %bitcast.3), custom_call_target="tpu_custom_call" | custom-call | tf_op jit(solution)/shard_map/pallas_call | solution.py:384
  43.2 0.6 %copy.7 = bf16[1,2,3584]{2,1,0:T(2,128)(2,1)} copy(bf16[1,2,3584]{2,1,0:T(2,128)(2,1)S(1)} %shard_map.48) | data formatting | bytes 28672
Async XLA Ops:
  0.7 0.7 %copy-start = (bf16[1,2,3584]{2,1,0:T(2,128)(2,1)S(1)}, bf16[1,2,3584]{2,1,0:T(2,128)(2,1)}, u32[]{:S(2)}) copy-start(bf16[1,2,3584]{2,1,0:T(2,128)(2,1)} %query_ref.1) | copy-start | bytes 43012
  1.4 0.7 %copy-start.1 = (s32[32]{0:T(128)S(1)}, s32[32]{0:T(128)}, u32[]{:S(2)}) copy-start(s32[32]{0:T(128)} %table_ref.1) | copy-start | bytes 388
where the time goes:
time: 44.3 us; the launch traced here: 43.8 us
  Pallas kernels  41.2 us (93%)
  local copies, waits for them, and re-layouts  1.96 us (4%)
  between operations  0.69 us (2%)
    pallas_call x1, Pallas kernels, body(): pl.pallas_call(functools.partial(attend_kernel, n, slots, width), out_sha...  15 us
    pallas_call x1, Pallas kernels, body(): pl.pallas_call(functools.partial(gather_kernel, n, width), out_shape=[eve...  13.9 us
    pallas_call x1, Pallas kernels, body(): pl.pallas_call(functools.partial(reduce_kernel, n), out_shape=jax.ShapeDt...  12.3 us
    unnamed x5, local copies, waits for them, and re-layouts  1.96 us

commit v1 on v0

--- a/solution.py
+++ b/solution.py
@@ -231,14 +231,12 @@
         limit = jnp.where(lane_row < ROWS, held_limit[indices[0]], held_limit[indices[1]])
         pair = jnp.concatenate([query_ref[at] for at in ats], axis=0).astype(jnp.float32)
         pair = jnp.transpose(pair)
-        scores = jnp.zeros((2 * BLOCK, HEAD), jnp.float32)
-        for r in range(2):
-            for k in range(0, KVH, 2):
-                block = jnp.concatenate([rows[k, indices[r]], rows[k + 1, indices[r]]], axis=1)
-                query = jnp.concatenate(
-                    [jnp.where(lane_group == r * KVH + h, pair, 0.0) for h in (k, k + 1)], axis=0
-                )
-                scores += jnp.dot(block, query.astype(jnp.bfloat16), preferred_element_type=jnp.float32)
+        heads = [(r, k) for r in range(2) for k in range(KVH)]
+        block = jnp.concatenate([rows[k, indices[r]] for r, k in heads], axis=1)
+        query = jnp.concatenate(
+            [jnp.where(lane_group == r * KVH + k, pair, 0.0).astype(jnp.bfloat16) for r, k in heads], axis=0
+        )
+        scores = jnp.dot(block, query, preferred_element_type=jnp.float32)
         scores = jnp.where(columns[...] < limit, scores * SCALE, MASKED)
         peak = jnp.maximum(jnp.max(scores, axis=0, keepdims=True), FLOOR)
         peak = peak.astype(jnp.bfloat16).astype(jnp.float32)
@@ -305,15 +303,15 @@
 
     def reduce_core(i):
         g.arrive(core_recv.at[i], core_s.at[i], core_r.at[i])
-        for d in list(range(1, PLANE)) + [0]:
-            p = g.plane_to[d]
-            state = encode(*merge([part_ref[g.line_from[i], g.c, p], core_recv[i, p]]))
-            if d == 0:
-                plane_own[i] = state
-            else:
-                plane_send[i, d - 1] = state.astype(jnp.bfloat16)
-                g.go(plane_send.at[i, d - 1], plane_recv.at[i, d - 1],
-                     plane_s.at[i, d - 1], plane_r.at[i, d - 1], g.plane(p))
+        states = [
+            encode(*merge([part_ref[g.line_from[i], g.c, p], core_recv[i, p]])) for p in g.plane_to
+        ]
+        plane_own[i] = states[0]
+        for d in range(1, PLANE):
+            plane_send[i, d - 1] = states[d].astype(jnp.bfloat16)
+        for d in range(1, PLANE):
+            g.go(plane_send.at[i, d - 1], plane_recv.at[i, d - 1],
+                 plane_s.at[i, d - 1], plane_r.at[i, d - 1], g.plane(g.plane_to[d]))
 
     def reduce_plane(i):
         for d in range(1, PLANE):

time: 44.3 us -> 44 us (level)
    pallas_call x1, Pallas kernels: 12.3 us -> 14.7 us  [body(): pl.pallas_call(functools.partial(reduce_kernel, n), out_shape=jax.ShapeDt...]
    pallas_call x1, Pallas kernels: 15 us -> 12.7 us  [body(): pl.pallas_call(functools.partial(attend_kernel, n, slots, width), out_sha...]
where the time goes in v1:
time: 44 us; the launch traced here: 43.9 us
  Pallas kernels  41.2 us (94%)
  local copies, waits for them, and re-layouts  1.96 us (4%)
  between operations  0.69 us (2%)
    pallas_call x1, Pallas kernels, body(): pl.pallas_call(functools.partial(reduce_kernel, n), out_shape=jax.ShapeDt...  14.7 us
    pallas_call x1, Pallas kernels, body(): pl.pallas_call(functools.partial(gather_kernel, n, width), out_shape=[eve...  13.9 us
    pallas_call x1, Pallas kernels, body(): pl.pallas_call(functools.partial(attend_kernel, n, slots, width), out_sha...  12.7 us
    unnamed x5, local copies, waits for them, and re-layouts  1.96 us

profile of v1, /device:TPU:0, one launch (start us, length us, event | category | flops | bytes accessed | tf_op | source)
XLA Modules:
  0.0 43.9 jit_solution(2074683457163893661)
XLA Ops:
  0.7 0.0 copy-start
  0.7 0.7 %copy-done = bf16[1,2,3584]{2,1,0:T(2,128)(2,1)S(1)} copy-done((bf16[1,2,3584]{2,1,0:T(2,128)(2,1)S(1)}, bf16[1,2,3584]{2,1,0:T(2,128)(2,1)}, u32[]{:S(2)}) %copy-start) | copy-done | bytes 14360
  1.4 0.0 copy-start.1
  1.4 0.7 %copy-done.1 = s32[32]{0:T(128)S(1)} copy-done((s32[32]{0:T(128)S(1)}, s32[32]{0:T(128)}, u32[]{:S(2)}) %copy-start.1) | copy-done | bytes 152
  2.0 13.9 %shard_map.46 = (bf16[4,2,4,64,128]{4,3,2,1,0:T(8,128)(2,1)S(1)}, s32[2,4,4,1,128]{4,3,2,1,0:T(1,128)S(1)}) custom-call(bf16[1,2,3584]{2,1,0:T(2,128)(2,1)S(1)} %copy-done, s32[1]{0:T(128)S(6)} %copy.6.lengths_ref, s32[32]{0:T(128)S(1)} %copy-done.1), custom_call_target="tpu_custom_call" | custom-call | tf_op jit(solution)/shard_map/pallas_call | solution.py:354
  15.9 12.7 %shard_map.47 = bf16[32,64,128]{2,1,0:T(8,128)(2,1)S(1)} custom-call(bf16[32,64,128]{2,1,0:T(8,128)(2,1)S(1)} %bitcast.4, s32[32,1,128]{2,1,0:T(1,128)S(1)} %bitcast.5, bf16[32,256,2,512]{3,2,1,0:T(2,128)(2,1)} %pool_ref.1), custom_call_target="tpu_custom_call" | custom-call | tf_op jit(solution)/shard_map/pallas_call | solution.py:368
  28.6 14.7 %shard_map.48 = bf16[1,2,3584]{2,1,0:T(2,128)(2,1)S(1)} custom-call(bf16[4,2,4,64,128]{4,3,2,1,0:T(8,128)(2,1)S(1)} %bitcast.3), custom_call_target="tpu_custom_call" | custom-call | tf_op jit(solution)/shard_map/pallas_call | solution.py:382
  43.3 0.6 %copy.7 = bf16[1,2,3584]{2,1,0:T(2,128)(2,1)} copy(bf16[1,2,3584]{2,1,0:T(2,128)(2,1)S(1)} %shard_map.48) | data formatting | bytes 28672
Async XLA Ops:
  0.7 0.7 %copy-start = (bf16[1,2,3584]{2,1,0:T(2,128)(2,1)S(1)}, bf16[1,2,3584]{2,1,0:T(2,128)(2,1)}, u32[]{:S(2)}) copy-start(bf16[1,2,3584]{2,1,0:T(2,128)(2,1)} %query_ref.1) | copy-start | bytes 43012
  1.4 0.7 %copy-start.1 = (s32[32]{0:T(128)S(1)}, s32[32]{0:T(128)}, u32[]{:S(2)}) copy-start(s32[32]{0:T(128)} %table_ref.1) | copy-start | bytes 388

commit v2 on v1

--- a/solution.py
+++ b/solution.py
@@ -18,6 +18,7 @@
 MASKED = -1e30
 FLOOR = -1e20
 UNROLL = 4
+KV_CHUNKS = 4
 SCALE = 1.0 / HEAD**0.5
 MESH = pl.DeviceIdType.MESH
 
@@ -87,21 +88,31 @@
 
 
 def gather_kernel(
-    n, width,
-    query_ref, lengths_ref, table_ref, every_query, meta,
-    spread, held_query, length_scalar, table_scalar, small_sem,
+    n, slots, width,
+    query_ref, lengths_ref, table_ref, pool_ref, every_query, meta, kv,
+    spread, held_query, length_scalar, table_scalar, small_sem, kv_sem,
     meta_line_s, meta_line_r, meta_plane_s, meta_plane_r, meta_core_s, meta_core_r,
     query_line_s, query_line_r, query_plane_s, query_plane_r, query_core_s, query_core_r,
 ):
     g = Grid(n)
     zz, pp, cc, depth = g.z, g.p, g.c, g.depth
     greeted = greet(g.peers())
+    chunk = slots // KV_CHUNKS
+    kv_copies = [
+        pltpu.make_async_copy(
+            pool_ref.at[pl.ds(part * chunk, chunk), :, :, pl.ds(k * HEAD, HEAD)],
+            kv.at[k, pl.ds(part * chunk, chunk)],
+            kv_sem.at[part, k],
+        )
+        for part in range(KV_CHUNKS)
+        for k in range(KVH)
+    ]
     small = [
         pltpu.make_async_copy(lengths_ref, length_scalar, small_sem.at[0]),
         pltpu.make_async_copy(table_ref, table_scalar, small_sem.at[1]),
         pltpu.make_async_copy(query_ref, held_query, small_sem.at[2]),
     ]
-    for copy in small:
+    for copy in small + kv_copies:
         copy.start()
 
     spread[...] = jnp.zeros_like(spread)
@@ -153,6 +164,8 @@
         g.arrive(every_query.at[g.line_from[i], g.other], query_core_s.at[i], query_core_r.at[i])
     g.arrive(meta.at[g.other], meta_core_s.at[0], meta_core_r.at[0])
     g.finish()
+    for copy in kv_copies:
+        copy.wait()
 
 
 def state_ids():
@@ -170,8 +183,8 @@
 
 def attend_kernel(
     n, slots, width,
-    query_ref, meta_ref, pool_ref, out_ref,
-    kv, columns, meta_scalar, held_at, held_limit, count_ref, kv_sem, scalar_sem,
+    query_ref, meta_ref, kv, out_ref,
+    columns, meta_scalar, held_at, held_slot, held_limit, count_ref, scalar_sem,
 ):
     me = lax.axis_index("pool")
     stride = n // width
@@ -195,14 +208,6 @@
 
     to_scalar.wait()
 
-    def pool_copies(index, slot):
-        return [
-            pltpu.make_async_copy(
-                pool_ref.at[slot, :, :, pl.ds(k * HEAD, HEAD)], kv.at[k, index], kv_sem.at[k, index]
-            )
-            for k in range(KVH)
-        ]
-
     count_ref[0] = 0
 
     @pl.loop(0, width)
@@ -216,8 +221,7 @@
             index = count_ref[0]
             held_at[index] = (z * CORES + c) * PLANE + p
             held_limit[index] = 2 * (length + 1 - place * BLOCK)
-            for copy in pool_copies(index, meta_scalar[line, 0, place] & (slots - 1)):
-                copy.start()
+            held_slot[index] = meta_scalar[line, 0, place] & (slots - 1)
             count_ref[0] = index + 1
 
     count = count_ref[0]
@@ -228,11 +232,12 @@
 
     def attend(indices):
         ats = [held_at[index] for index in indices]
+        held = [held_slot[index] for index in indices]
         limit = jnp.where(lane_row < ROWS, held_limit[indices[0]], held_limit[indices[1]])
         pair = jnp.concatenate([query_ref[at] for at in ats], axis=0).astype(jnp.float32)
         pair = jnp.transpose(pair)
         heads = [(r, k) for r in range(2) for k in range(KVH)]
-        block = jnp.concatenate([rows[k, indices[r]] for r, k in heads], axis=1)
+        block = jnp.concatenate([rows[k, held[r]] for r, k in heads], axis=1)
         query = jnp.concatenate(
             [jnp.where(lane_group == r * KVH + k, pair, 0.0).astype(jnp.bfloat16) for r, k in heads], axis=0
         )
@@ -248,7 +253,7 @@
         for r in range(2):
             numers = []
             for k in range(0, KVH, 2):
-                block = jnp.concatenate([rows[k, indices[r]], rows[k + 1, indices[r]]], axis=1)
+                block = jnp.concatenate([rows[k, held[r]], rows[k + 1, held[r]]], axis=1)
                 base = r * ROWS + 16 * k
                 both = jnp.dot(weights[base : base + 32], block, preferred_element_type=jnp.float32)
                 numers += [both[:16, :HEAD], both[16:, HEAD:]]
@@ -260,14 +265,6 @@
 
     @pl.loop(0, (count + UNROLL - 1) // UNROLL)
     def _(step):
-        for u in range(UNROLL):
-            index = step * UNROLL + u
-
-            @pl.when(index < count)
-            def _():
-                for copy in pool_copies(index, 0):
-                    copy.wait()
-
         indices = [jnp.minimum(step * UNROLL + u, count - 1) for u in range(UNROLL)]
         done = [attend(indices[u : u + 2]) for u in range(0, UNROLL, 2)]
         for at, state in sum(done, []):
@@ -349,36 +346,39 @@
     meta_shape = (CORES, PLANE, depth, 1, HEAD)
 
     def params(**more):
-        return pltpu.CompilerParams(has_side_effects=True, vmem_limit_bytes=48 * 1024 * 1024, **more)
-
-    every_query, meta = pl.pallas_call(
-        functools.partial(gather_kernel, n, width),
-        out_shape=[every, jax.ShapeDtypeStruct(meta_shape, i32)],
-        in_specs=[far, far, far],
-        out_specs=[vmem, vmem],
+        return pltpu.CompilerParams(has_side_effects=True, vmem_limit_bytes=28 * 1024 * 1024, **more)
+
+    every_query, meta, kv = pl.pallas_call(
+        functools.partial(gather_kernel, n, slots, width),
+        out_shape=[
+            every,
+            jax.ShapeDtypeStruct(meta_shape, i32),
+            jax.ShapeDtypeStruct((KVH, slots, BLOCK, 2, HEAD), bf16),
+        ],
+        in_specs=[far, far, far, anywhere],
+        out_specs=[vmem, vmem, vmem],
         scratch_shapes=[
             pltpu.VMEM(state, f32), pltpu.VMEM(queries.shape, bf16),
-            pltpu.SMEM((1,), i32), pltpu.SMEM((width,), i32), dma((3,)),
+            pltpu.SMEM((1,), i32), pltpu.SMEM((width,), i32), dma((3,)), dma((KV_CHUNKS, KVH)),
             dma((depth - 1,)), dma((depth - 1,)), dma((PLANE - 1,)), dma((PLANE - 1,)), dma((1,)), dma((1,)),
             dma((depth - 1,)), dma((depth - 1,)), dma((depth, PLANE - 1)), dma((depth, PLANE - 1)),
             dma((depth,)), dma((depth,)),
         ],
         compiler_params=params(collective_id=0),
-    )(queries, lengths, block_table)
+    )(queries, lengths, block_table, kv_pool)
     parts = pl.pallas_call(
         functools.partial(attend_kernel, n, slots, width),
         out_shape=jax.ShapeDtypeStruct((n,) + state, bf16),
-        in_specs=[vmem, anywhere, anywhere],
+        in_specs=[vmem, anywhere, vmem],
         out_specs=vmem,
         scratch_shapes=[
-            pltpu.VMEM((KVH, slots, BLOCK, 2, HEAD), bf16),
             pltpu.VMEM((2 * BLOCK, HEAD), i32),
             pltpu.SMEM((n, 1, HEAD), i32),
-            pltpu.SMEM((width,), i32), pltpu.SMEM((width,), i32), pltpu.SMEM((1,), i32),
-            dma((KVH, slots)), dma,
+            pltpu.SMEM((width,), i32), pltpu.SMEM((width,), i32), pltpu.SMEM((width,), i32),
+            pltpu.SMEM((1,), i32), dma,
         ],
         compiler_params=params(),
-    )(every_query.reshape((n,) + state), meta.reshape(n, 1, HEAD), kv_pool)
+    )(every_query.reshape((n,) + state), meta.reshape(n, 1, HEAD), kv)
     return pl.pallas_call(
         functools.partial(reduce_kernel, n),
         out_shape=jax.ShapeDtypeStruct(queries.shape, queries.dtype),

time: 44 us -> 42.1 us (0.957)
  Pallas kernels: 41.2 us -> 38.9 us
    pallas_call x1, Pallas kernels: 14.7 us -> 12.2 us  [body(): pl.pallas_call(functools.partial(reduce_kernel, n), out_shape=jax.ShapeDt...]
where the time goes in v2:
time: 42.1 us; the launch traced here: 41.6 us
  Pallas kernels  38.9 us (92%)
  local copies, waits for them, and re-layouts  1.96 us (5%)
  between operations  0.69 us (2%)
    pallas_call x1, Pallas kernels, body(): pl.pallas_call(functools.partial(gather_kernel, n, slots, width), out_sha...  14 us
    pallas_call x1, Pallas kernels, body(): pl.pallas_call(functools.partial(attend_kernel, n, slots, width), out_sha...  12.7 us
    pallas_call x1, Pallas kernels, body(): pl.pallas_call(functools.partial(reduce_kernel, n), out_shape=jax.ShapeDt...  12.2 us
    unnamed x5, local copies, waits for them, and re-layouts  1.96 us

profile of v2, /device:TPU:0, one launch (start us, length us, event | category | flops | bytes accessed | tf_op | source)
XLA Modules:
  0.0 41.6 jit_solution(3755532876271637303)
XLA Ops:
  0.7 0.0 copy-start
  0.7 0.7 %copy-done = bf16[1,2,3584]{2,1,0:T(2,128)(2,1)S(1)} copy-done((bf16[1,2,3584]{2,1,0:T(2,128)(2,1)S(1)}, bf16[1,2,3584]{2,1,0:T(2,128)(2,1)}, u32[]{:S(2)}) %copy-start) | copy-done | bytes 14360
  1.4 0.0 copy-start.1
  1.4 0.7 %copy-done.1 = s32[32]{0:T(128)S(1)} copy-done((s32[32]{0:T(128)S(1)}, s32[32]{0:T(128)}, u32[]{:S(2)}) %copy-start.1) | copy-done | bytes 152
  2.0 14.0 %shard_map.46 = (bf16[4,2,4,64,128]{4,3,2,1,0:T(8,128)(2,1)S(1)}, s32[2,4,4,1,128]{4,3,2,1,0:T(1,128)S(1)}, bf16[4,32,256,2,128]{4,3,2,1,0:T(2,128)(2,1)S(1)}) custom-call(bf16[1,2,3584]{2,1,0:T(2,128)(2,1)S(1)} %copy-done, s32[1]{0:T(128)S(6)} %copy.6.lengths_ref, s32[32]{0:T(128)S(1)} %copy-done.1, bf16[32,256,2,512]{3,2,1,0:T(2,128)(2,1)} %pool_ref.1), custom_call_target="tpu_custom_call" | custom-call | tf_op jit(solution)/shard_map/pallas_call | solution.py:351
  16.1 12.7 %shard_map.47 = bf16[32,64,128]{2,1,0:T(8,128)(2,1)S(1)} custom-call(bf16[32,64,128]{2,1,0:T(8,128)(2,1)S(1)} %bitcast.4, s32[32,1,128]{2,1,0:T(1,128)S(1)} %bitcast.5, bf16[4,32,256,2,128]{4,3,2,1,0:T(2,128)(2,1)S(1)} %get-tuple-element.10.kv), custom_call_target="tpu_custom_call" | custom-call | tf_op jit(solution)/shard_map/pallas_call | solution.py:369
  28.7 12.2 %shard_map.48 = bf16[1,2,3584]{2,1,0:T(2,128)(2,1)S(1)} custom-call(bf16[4,2,4,64,128]{4,3,2,1,0:T(8,128)(2,1)S(1)} %bitcast.3), custom_call_target="tpu_custom_call" | custom-call | tf_op jit(solution)/shard_map/pallas_call | solution.py:382
  41.0 0.6 %copy.7 = bf16[1,2,3584]{2,1,0:T(2,128)(2,1)} copy(bf16[1,2,3584]{2,1,0:T(2,128)(2,1)S(1)} %shard_map.48) | data formatting | bytes 28672
Async XLA Ops:
  0.7 0.7 %copy-start = (bf16[1,2,3584]{2,1,0:T(2,128)(2,1)S(1)}, bf16[1,2,3584]{2,1,0:T(2,128)(2,1)}, u32[]{:S(2)}) copy-start(bf16[1,2,3584]{2,1,0:T(2,128)(2,1)} %query_ref.1) | copy-start | bytes 43012
  1.4 0.7 %copy-start.1 = (s32[32]{0:T(128)S(1)}, s32[32]{0:T(128)}, u32[]{:S(2)}) copy-start(s32[32]{0:T(128)} %table_ref.1) | copy-start | bytes 388

commit v3 on v2

--- a/solution.py
+++ b/solution.py
@@ -17,7 +17,7 @@
 M_ROW, L_ROW, L_LOW_ROW = 14, 15, 30
 MASKED = -1e30
 FLOOR = -1e20
-UNROLL = 4
+UNROLL = 2
 KV_CHUNKS = 4
 SCALE = 1.0 / HEAD**0.5
 MESH = pl.DeviceIdType.MESH

time: 42.1 us -> 41.1 us (0.976); the launches traced: 41.6 us -> 41.3 us
  no operation moved by 1% of the time
where the time goes in v3:
time: 41.1 us; the launch traced here: 41.3 us
  Pallas kernels  38.7 us (94%)
  local copies, waits for them, and re-layouts  1.96 us (5%)
  between operations  0.69 us (2%)
    pallas_call x1, Pallas kernels, body(): pl.pallas_call(functools.partial(gather_kernel, n, slots, width), out_sha...  14 us
    pallas_call x1, Pallas kernels, body(): pl.pallas_call(functools.partial(attend_kernel, n, slots, width), out_sha...  12.7 us
    pallas_call x1, Pallas kernels, body(): pl.pallas_call(functools.partial(reduce_kernel, n), out_shape=jax.ShapeDt...  11.9 us
    unnamed x5, local copies, waits for them, and re-layouts  1.96 us

profile of v3, /device:TPU:0, one launch (start us, length us, event | category | flops | bytes accessed | tf_op | source)
XLA Modules:
  0.0 41.3 jit_solution(11734790162135547840)
XLA Ops:
  0.7 0.0 copy-start
  0.7 0.7 %copy-done = bf16[1,2,3584]{2,1,0:T(2,128)(2,1)S(1)} copy-done((bf16[1,2,3584]{2,1,0:T(2,128)(2,1)S(1)}, bf16[1,2,3584]{2,1,0:T(2,128)(2,1)}, u32[]{:S(2)}) %copy-start) | copy-done | bytes 14360
  1.4 0.0 copy-start.1
  1.4 0.7 %copy-done.1 = s32[32]{0:T(128)S(1)} copy-done((s32[32]{0:T(128)S(1)}, s32[32]{0:T(128)}, u32[]{:S(2)}) %copy-start.1) | copy-done | bytes 152
  2.0 14.0 %shard_map.46 = (bf16[4,2,4,64,128]{4,3,2,1,0:T(8,128)(2,1)S(1)}, s32[2,4,4,1,128]{4,3,2,1,0:T(1,128)S(1)}, bf16[4,32,256,2,128]{4,3,2,1,0:T(2,128)(2,1)S(1)}) custom-call(bf16[1,2,3584]{2,1,0:T(2,128)(2,1)S(1)} %copy-done, s32[1]{0:T(128)S(6)} %copy.6.lengths_ref, s32[32]{0:T(128)S(1)} %copy-done.1, bf16[32,256,2,512]{3,2,1,0:T(2,128)(2,1)} %pool_ref.1), custom_call_target="tpu_custom_call" | custom-call | tf_op jit(solution)/shard_map/pallas_call | solution.py:351
  16.1 12.7 %shard_map.47 = bf16[32,64,128]{2,1,0:T(8,128)(2,1)S(1)} custom-call(bf16[32,64,128]{2,1,0:T(8,128)(2,1)S(1)} %bitcast.4, s32[32,1,128]{2,1,0:T(1,128)S(1)} %bitcast.5, bf16[4,32,256,2,128]{4,3,2,1,0:T(2,128)(2,1)S(1)} %get-tuple-element.10.kv), custom_call_target="tpu_custom_call" | custom-call | tf_op jit(solution)/shard_map/pallas_call | solution.py:369
  28.8 11.9 %shard_map.48 = bf16[1,2,3584]{2,1,0:T(2,128)(2,1)S(1)} custom-call(bf16[4,2,4,64,128]{4,3,2,1,0:T(8,128)(2,1)S(1)} %bitcast.3), custom_call_target="tpu_custom_call" | custom-call | tf_op jit(solution)/shard_map/pallas_call | solution.py:382
  40.7 0.6 %copy.7 = bf16[1,2,3584]{2,1,0:T(2,128)(2,1)} copy(bf16[1,2,3584]{2,1,0:T(2,128)(2,1)S(1)} %shard_map.48) | data formatting | bytes 28672
Async XLA Ops:
  0.7 0.7 %copy-start = (bf16[1,2,3584]{2,1,0:T(2,128)(2,1)S(1)}, bf16[1,2,3584]{2,1,0:T(2,128)(2,1)}, u32[]{:S(2)}) copy-start(bf16[1,2,3584]{2,1,0:T(2,128)(2,1)} %query_ref.1) | copy-start | bytes 43012
  1.4 0.7 %copy-start.1 = (s32[32]{0:T(128)S(1)}, s32[32]{0:T(128)}, u32[]{:S(2)}) copy-start(s32[32]{0:T(128)} %table_ref.1) | copy-start | bytes 388
